TPU v7x, 128 devices: a whole 4x4x4 slice. The times are simulated.
128 devices in a mesh: grp: 4 (over y_hi, core), dev: 32 (over x, y_lo, z).
Axes of the slice: x: 4, y: 4 (y_hi: 2, y_lo: 2; y = y_hi * 2 + y_lo), z: 4, core: 2. Of those that a mesh axis runs over, the one named last changes fastest.
Arguments:
- grad_parts: float32 [4, 2, 32, 1024, 1024], P('grp', None, 'dev'), may hold values from -4 to 4
- light_parts: float32 [4, 1024, 1024], P('grp'), may hold values from 0.1 to 1
- object_field: float32 [2, 32, 1024, 1024], P(None, 'dev', 'grp'), may hold values from -4 to 4
Outputs:
- updated: float32 [2, 32, 1024, 1024], P(None, 'dev', 'grp')
All inputs are finite; a program needn't handle non-finite values.
Results may differ from a plain program's by a relative error of at most 0.000073.
Values sent between devices are 32-bit elements; how exact they have to be, the bound alone decides.
A program may use at most 128 MiB of HBM per device.

v0:
```python
import math

import jax
import jax.numpy as jnp
from jax import lax
from jax.sharding import PartitionSpec as P

damping = 0.05
ceiling = 0.4


def mixing_matrix(count):
    wavenumber = jnp.arange(count, dtype=jnp.int32)
    signed = jnp.where(2 * wavenumber < count, wavenumber, wavenumber - count).astype(jnp.float32)
    taper = jnp.exp(-((signed / (count / 8.0)) ** 2))
    offsets = (wavenumber[:, None] - wavenumber[None, :]) % count
    phases = wavenumber[None, None, :] * offsets[:, :, None] % count
    angles = 2.0 * math.pi / count * phases.astype(jnp.float32)
    return jnp.sum(taper * jnp.cos(angles), axis=2) / count


def regularize(block):
    shape = block.shape
    flattened = block.reshape(2, shape[1], -1)
    mixed = jnp.einsum(
        "zs,csm->czm", mixing_matrix(shape[1]), flattened, precision=lax.Precision.HIGHEST
    )
    amplitude = jnp.sqrt(mixed[0] * mixed[0] + mixed[1] * mixed[1])
    factor = ceiling / jnp.maximum(amplitude, ceiling)
    return (mixed * factor[None]).reshape(shape)


def return_slabs(block):
    return lax.all_to_all(block, "dev", split_axis=1, concat_axis=2, tiled=True)


def per_device(grad_parts, light_parts, object_field):
    ndevices = lax.axis_size("dev")
    slab = object_field.shape[1]
    quarter = object_field.shape[2]
    width = object_field.shape[3]
    rowcount = quarter // ndevices
    partial_grad = grad_parts.reshape(2, slab, -1, width)
    partial_light = light_parts.reshape(-1, width)
    gradient, lighting = (
        lax.psum_scatter(partial_grad, "grp", scatter_dimension=2, tiled=True),
        lax.psum_scatter(partial_light, "grp", scatter_dimension=0, tiled=True),
    )
    stepped = object_field - gradient / (lighting[None, None] + damping)
    blocks = stepped.reshape(2, slab, ndevices, rowcount, width)
    result = return_slabs(
        regularize(lax.all_to_all(blocks, "dev", split_axis=2, concat_axis=1, tiled=True))
    )
    return result.reshape(2, slab, quarter, width)


def solution(mesh):
    in_specs = (
        P("grp", None, "dev", None, None),
        P("grp", None, None),
        P(None, "dev", "grp", None),
    )
    out_specs = P(None, "dev", "grp", None)
    return jax.shard_map(
        per_device, mesh=mesh, in_specs=in_specs, out_specs=out_specs, check_vma=False
    )
```

profile of v0, /device:TPU:0, one launch (start us, length us, event | category | flops | bytes accessed | tf_op | source)
XLA Modules:
  0.0 234.1 jit_solution(14444269370658387415)
XLA Ops:
  6.5 0.0 reduce-scatter.5.cloned.1.call-start
  6.5 0.7 reduce-scatter.5.cloned.1.call-update
  7.3 0.0 reduce-scatter.3.cloned.1.call-start
  7.3 0.7 reduce-scatter.3.cloned.1.call-update
  8.0 0.0 copy-start
  8.0 55.9 %reduce-scatter.5.cloned.1.call-done = f32[256,1024]{1,0:T(8,128)} async-done(((f32[1024,1024]{1,0:T(8,128)}), f32[256,1024]{1,0:T(8,128)}) %reduce-scatter.5.cloned.1.call-update) | async-done | bytes 1048592 | tf_op jit(solution)/shard_map/reduce_scatter | solution.py:47
  63.9 1.3 broadcast_add_fusion
  65.2 79.6 %reduce-scatter.3.cloned.1.call-done = f32[2,1,256,1024]{3,2,0,1:T(8,128)} async-done(((f32[2,1,1024,1024]{3,2,0,1:T(8,128)}), f32[2,1,256,1024]{3,2,0,1:T(8,128)}) %reduce-scatter.3.cloned.1.call-update) | async-done | bytes 2097168 | tf_op jit(solution)/shard_map/reduce_scatter | solution.py:46
  144.9 0.0 copy-done
  144.9 2.1 fusion.1
  147.0 1.6 copy.13
  148.6 7.3 %all-to-all-start = ((f32[2,1,32,8,1024]{4,3,0,1,2:T(8,128)}), f32[2,1,32,8,1024]{4,3,0,1,2:T(8,128)S(1)}, u32[]{:S(2)}, u32[]{:S(2)}) async-start(f32[2,1,32,8,1024]{4,3,0,1,2:T(8,128)} %copy.13), calls=%async_computation.2 | async-start | bytes 4194304 | tf_op jit(solution)/shard_map/all_to_all | solution.py:52
  155.9 2.2 fusion.12
  158.1 25.7 %all-to-all-done = f32[2,1,32,8,1024]{4,3,0,1,2:T(8,128)S(1)} async-done(((f32[2,1,32,8,1024]{4,3,0,1,2:T(8,128)}), f32[2,1,32,8,1024]{4,3,0,1,2:T(8,128)S(1)}, u32[]{:S(2)}, u32[]{:S(2)}) %all-to-all-start) | async-done | bytes 2097184 | tf_op jit(solution)/shard_map/all_to_all | solution.py:52
  183.8 2.8 %reshape.74 = f32[2,32,8192]{2,0,1:T(2,128)} reshape(f32[2,1,32,8,1024]{4,3,0,1,2:T(8,128)S(1)} %all-to-all-done) | data formatting | bytes 4194304 | tf_op jit(solution)/shard_map/reshape | solution.py:24
  186.6 4.7 %convolution_bitcast_fusion = f32[2,32,8192]{2,1,0:T(8,128)S(1)} fusion(f32[2,32,8192]{2,0,1:T(2,128)} %reshape.74, f32[32,32]{1,0:T(8,128)S(1)} %fusion.12), kind=kOutput, calls=%fused_computation | convolution fusion | flops 201327616 | bytes 4198400 | tf_op jit(solution)/shard_map/zs,csm->czm/dot_general | solution.py:25
  191.3 0.5 fusion.6
  191.7 0.2 broadcast_multiply_fusion
  191.9 1.2 copy.19
  193.1 0.2 copy.15
  193.4 32.4 %all_to_all.8 = f32[2,32,1,8,1024]{4,3,0,2,1:T(8,128)S(1)} all-to-all(f32[2,32,1,8,1024]{4,3,0,2,1:T(8,128)S(1)} %copy.15), channel_id=1, replica_groups=mesh['grp'=4,'dev'=32] {'dev'}, dimensions={1} | all-to-all | bytes 4194304 | tf_op jit(solution)/shard_map/all_to_all | solution.py:34
  225.8 1.5 copy.23
  (2 shorter events, 0.0 us)
Async XLA Ops:
  6.5 57.4 %reduce-scatter.5.cloned.1.call-start = ((), (), s32[]{:S(2)}) async-start(), calls=%async_computation.5 | async-start | bytes 5242880 | tf_op jit(solution)/shard_map/reduce_scatter | solution.py:47
  7.3 137.6 %reduce-scatter.3.cloned.1.call-start = ((), (), s32[]{:S(2)}) async-start(), calls=%async_computation.4 | async-start | bytes 10485760 | tf_op jit(solution)/shard_map/reduce_scatter | solution.py:46
  8.0 136.9 %copy-start = (f32[2,1,256,1024]{3,2,1,0:T(8,128)S(1)}, f32[2,1,256,1024]{3,2,1,0:T(8,128)}, u32[]{:S(2)}) copy-start(f32[2,1,256,1024]{3,2,1,0:T(8,128)} %param.5) | copy-start | bytes 6291460
  148.6 35.2 %all-to-all-start = ((f32[2,1,32,8,1024]{4,3,0,1,2:T(8,128)}), f32[2,1,32,8,1024]{4,3,0,1,2:T(8,128)S(1)}, u32[]{:S(2)}, u32[]{:S(2)}) async-start(f32[2,1,32,8,1024]{4,3,0,1,2:T(8,128)} %copy.13), calls=%async_computation.2 | async-start | bytes 4194304 | tf_op jit(solution)/shard_map/all_to_all | solution.py:52
Sparse Core Ops, SparseCore 0:
  10.0 53.8 reduce-scatter.4
  66.8 78.0 reduce-scatter.2
where the time goes:
time: 234 us
  waiting for transfers between devices  163 us (70%)
  blocking collectives  32.4 us (14%)
  between operations  13.5 us (6%)
  starting transfers between devices  7.32 us (3%)
  local copies, waits for them, and re-layouts  7.22 us (3%)
  other arithmetic  6.35 us (3%)
  matrix products  4.71 us (2%)
    reduce_scatter x1, waiting for transfers between devices, per_device(): lax.psum_scatter(partial_grad, 'grp', scatter_dimension=2, tiled=True)  79.6 us
    reduce_scatter x1, waiting for transfers between devices, per_device(): lax.psum_scatter(partial_light, 'grp', scatter_dimension=0, tiled=True)  55.9 us
    all_to_all x1, blocking collectives, return_slabs(): return lax.all_to_all(block, 'dev', split_axis=1, concat_axis=2, tiled=True)  32.4 us
    all_to_all x1, waiting for transfers between devices, per_device(): lax.all_to_all(blocks, 'dev', split_axis=2, concat_axis=1, tiled=True)  25.7 us
    all_to_all x1, starting transfers between devices, per_device(): lax.all_to_all(blocks, 'dev', split_axis=2, concat_axis=1, tiled=True)  7.28 us
    dot_general x1, matrix products, regularize(): jnp.einsum('zs,csm->czm', mixing_matrix(shape[1]), flattened, precision=l...  4.71 us
  transfers between devices with their start and end apart: 3, of which 3 were waited for; matrix products, arithmetic and copies ran while one was open for 2% of the time, Pallas kernels for 0%

commit v1 on v0

v1 whole, which is shorter than its diff:
```python
import functools
import math

import jax
import jax.numpy as jnp
import numpy as np
from jax import lax
from jax.experimental import pallas as pl
from jax.experimental.pallas import tpu as pltpu
from jax.sharding import PartitionSpec as P

damping = 0.05
ceiling = 0.4
MESH = pl.DeviceIdType.MESH
CHUNKS = 4


def mixing_matrix(count, lanes):
    wavenumber = np.arange(count)
    signed = np.where(2 * wavenumber < count, wavenumber, wavenumber - count)
    taper = np.exp(-((signed / (count / 8.0)) ** 2))
    offsets = (wavenumber[:, None] - wavenumber[None, :]) % count
    angles = 2.0 * math.pi / count * ((wavenumber[None, None, :] * offsets[:, :, None]) % count)
    mixing = np.sum(taper * np.cos(angles), axis=2) / count
    return np.kron(mixing, np.eye(lanes)).astype(np.float32)


def wait_for(ref, sem):
    pltpu.make_async_copy(ref, ref, sem).wait()


def kernel(
    mix_ref, grad, light, field, out,
    pbuf, cbuf, obuf, lbuf, dbuf, from_a, from_b, from_d, sbuf, xbuf, ybuf,
    load_sem, field_sem, core_send, core_recv, light_send, light_recv, damp_send, damp_recv,
    y_send, y_recv, plane_send, plane_recv, back_send, back_recv,
):
    width = pbuf.shape[-1]
    g = lax.axis_index("grp")
    me = lax.axis_index("dev")
    yh, core = lax.div(g, 2), lax.rem(g, 2)
    x, yl, z = lax.div(me, 8), lax.rem(lax.div(me, 4), 2), lax.rem(me, 4)
    place = x * 4 + z
    other_half = (1 - yh) * 2

    sibling = (yh * 2 + 1 - core, me)
    a_side = (g, x * 8 + (1 - yl) * 4 + z)
    b_side = (other_half + core, x * 8 + (1 - yl) * 4 + z)
    b_cross = (other_half + 1 - core, x * 8 + (1 - yl) * 4 + z)
    d_side = (other_half + core, me)

    def plane_peer(i):
        px = lax.rem(x + lax.div(i, 4), 4)
        pz = lax.rem(z + lax.rem(i, 4), 4)
        return px, pz

    def columns(k):
        return pl.ds(pl.multiple_of(k * width, width), width)

    def remote(src, dst, send, recv, target):
        pltpu.make_async_remote_copy(
            src_ref=src, dst_ref=dst, send_sem=send, recv_sem=recv,
            device_id=target, device_id_type=MESH,
        ).start()

    rows16 = pl.ds(pl.multiple_of(place * 16, 16), 16)
    pltpu.make_async_copy(light.at[yh, core, rows16], lbuf.at[0], light_recv).start()
    for k in range(CHUNKS):
        pltpu.make_async_copy(
            grad.at[:, :, core, :, columns(k)], pbuf.at[k], load_sem.at[k]
        ).start()
    for k in range(CHUNKS):
        pltpu.make_async_copy(field.at[:, :, columns(k)], obuf.at[k], field_sem.at[k]).start()

    barrier = pltpu.get_barrier_semaphore()
    for target in (sibling, b_side, b_cross, d_side):
        pl.semaphore_signal(barrier, 1, device_id=target, device_id_type=MESH)

    def greet(i, carry):
        pl.semaphore_signal(
            barrier, 1, device_id=(g, lax.rem(me + i, 32)), device_id_type=MESH
        )
        return carry

    lax.fori_loop(1, 32, greet, 0)
    pl.semaphore_wait(barrier, 35)

    remote(light.at[yh, 1 - core, rows16], lbuf.at[1], light_send, light_recv, sibling)
    remote(light.at[1 - yh, core, rows16], lbuf.at[2], light_send, light_recv, b_side)
    remote(light.at[1 - yh, 1 - core, rows16], lbuf.at[3], light_send, light_recv, b_cross)

    for k in range(CHUNKS):
        remote(
            grad.at[:, :, 1 - core, :, columns(k)], cbuf.at[k],
            core_send, core_recv.at[k], sibling,
        )

    wait_for(lbuf, light_recv)

    for k in range(CHUNKS):
        cols = pl.ds(k * width, width)
        dbuf[k, rows16, :] = (
            lbuf[0, :, cols] + lbuf[1, :, cols] + lbuf[2, :, cols] + lbuf[3, :, cols] + damping
        )

    def spread(n, carry):
        k, i = lax.div(n, 15), lax.rem(n, 15) + 1
        px, pz = plane_peer(i)
        remote(
            dbuf.at[k, rows16], dbuf.at[k, rows16], damp_send, damp_recv.at[k],
            (g, px * 8 + yl * 4 + pz),
        )
        return carry

    lax.fori_loop(0, 15 * CHUNKS, spread, 0)

    mine = pl.ds(pl.multiple_of(yl * 128, 128), 128)
    theirs = pl.ds(pl.multiple_of((1 - yl) * 128, 128), 128)

    def chip_sum(k, carry):
        wait_for(pbuf.at[k], load_sem.at[k])
        wait_for(cbuf.at[k], core_recv.at[k])
        pbuf[k] = pbuf[k] + cbuf[k]
        remote(pbuf.at[k, :, 1 - yh, mine], from_d.at[k], y_send.at[0], y_recv.at[0, k], d_side)
        remote(pbuf.at[k, :, 1 - yh, theirs], from_b.at[k], y_send.at[1], y_recv.at[1, k], b_side)
        return carry

    lax.fori_loop(0, CHUNKS, chip_sum, 0)

    def send_near(k, carry):
        wait_for(obuf.at[k], field_sem.at[k])
        wait_for(dbuf.at[k, pl.ds(0, 240)], damp_recv.at[k])
        damp = dbuf[k, theirs, :]
        pbuf[k, :, yh, theirs] = obuf[k, :, theirs, :] * damp[None] - pbuf[k, :, yh, theirs]
        remote(pbuf.at[k, :, yh, theirs], from_a.at[k], y_send.at[2], y_recv.at[2, k], a_side)
        return carry

    lax.fori_loop(0, CHUNKS, send_near, 0)

    def send_plane(k):
        wait_for(from_d.at[k], y_recv.at[0, k])
        damp = dbuf[k, mine, :]
        sbuf[k, :, yl] = obuf[k, :, mine, :] * damp[None] - pbuf[k, :, yh, mine] - from_d[k]
        wait_for(from_b.at[k], y_recv.at[1, k])
        wait_for(from_a.at[k], y_recv.at[2, k])
        sbuf[k, :, 1 - yl] = from_a[k] - from_b[k]

        def send(i, carry):
            px, pz = plane_peer(i)
            rows = pl.ds(pl.multiple_of((px * 4 + pz) * 8, 8), 8)
            remote(
                sbuf.at[k, :, :, rows], xbuf.at[k, :, x, :, z], plane_send, plane_recv.at[k],
                (g, px * 8 + yl * 4 + pz),
            )
            return carry

        lax.fori_loop(1, 16, send, 0)
        own = pl.ds(pl.multiple_of(place * 8, 8), 8)
        pltpu.make_async_copy(
            sbuf.at[k, :, :, own], xbuf.at[k, :, x, :, z], plane_recv.at[k]
        ).start()

    own_rows = pl.ds(pl.multiple_of(yl * 128 + place * 8, 8), 8)

    def mix_and_return(k):
        wait_for(xbuf.at[k], plane_recv.at[k])
        inverse = 1.0 / dbuf[k, own_rows, :]
        for part in range(2):
            block = xbuf[k, part].reshape(256, width)
            mixed = jnp.dot(
                mix_ref[...], block, precision=lax.Precision.HIGHEST,
                preferred_element_type=jnp.float32,
            )
            ybuf[k, part] = mixed.reshape(32, 8, width) * inverse[None]

        def send(i, carry):
            target = lax.rem(me + i, 32)
            remote(
                ybuf.at[k, :, target], out.at[:, own_rows, columns(k)], back_send, back_recv,
                (g, target),
            )
            return carry

        lax.fori_loop(1, 32, send, 0)
        pltpu.make_async_copy(
            ybuf.at[k, :, me], out.at[:, own_rows, columns(k)], back_recv
        ).start()

    send_plane(0)

    def steady(k, carry):
        send_plane(k)
        mix_and_return(k - 1)
        return carry

    lax.fori_loop(1, CHUNKS, steady, 0)
    mix_and_return(CHUNKS - 1)

    wait_for(lbuf.at[pl.ds(0, 3)], light_send)
    wait_for(cbuf, core_send)
    wait_for(dbuf.at[:, pl.ds(0, 240)], damp_send)
    wait_for(from_d, y_send.at[0])
    wait_for(from_b, y_send.at[1])
    wait_for(from_a, y_send.at[2])
    wait_for(sbuf.at[:, :, :, pl.ds(0, 120)], plane_send)
    wait_for(ybuf.at[:, :, pl.ds(0, 31)], back_send)
    wait_for(out, back_recv)


def per_device(grad_parts, light_parts, object_field):
    rows, columns = light_parts.shape[1:]
    slices = 32
    quarter = rows // 4
    width = columns // CHUNKS
    f32 = jnp.float32
    grad = grad_parts.reshape(2, 2, 2, quarter, columns)
    light = light_parts.reshape(2, 2, quarter, columns)
    field = object_field.reshape(2, quarter, columns)
    any_space = pl.BlockSpec(memory_space=pl.ANY)
    dma = pltpu.SemaphoreType.DMA
    half = quarter // 2
    mixed = pl.pallas_call(
        kernel,
        out_shape=jax.ShapeDtypeStruct((2, quarter, columns), f32),
        in_specs=[pl.BlockSpec(memory_space=pltpu.VMEM), any_space, any_space, any_space],
        out_specs=any_space,
        scratch_shapes=[
            pltpu.VMEM((CHUNKS, 2, 2, quarter, width), f32),
            pltpu.VMEM((CHUNKS, 2, 2, quarter, width), f32),
            pltpu.VMEM((CHUNKS, 2, quarter, width), f32),
            pltpu.VMEM((4, 16, columns), f32),
            pltpu.VMEM((CHUNKS, quarter, width), f32),
            pltpu.VMEM((CHUNKS, 2, half, width), f32),
            pltpu.VMEM((CHUNKS, 2, half, width), f32),
            pltpu.VMEM((CHUNKS, 2, half, width), f32),
            pltpu.VMEM((CHUNKS, 2, 2, half, width), f32),
            pltpu.VMEM((CHUNKS, 2, 4, 2, 4, 8, width), f32),
            pltpu.VMEM((CHUNKS, 2, slices, 8, width), f32),
            dma((CHUNKS,)), dma((CHUNKS,)),
            dma, dma((CHUNKS,)),
            dma, dma,
            dma, dma((CHUNKS,)),
            dma((3,)), dma((3, CHUNKS)),
            dma, dma((CHUNKS,)),
            dma, dma,
        ],
        compiler_params=pltpu.CompilerParams(
            collective_id=0, has_side_effects=True, vmem_limit_bytes=48 * 2**20
        ),
    )(jnp.asarray(mixing_matrix(slices, 8)), grad, light, field)
    amplitude = jnp.sqrt(mixed[0] * mixed[0] + mixed[1] * mixed[1])
    factor = ceiling / jnp.maximum(amplitude, ceiling)
    return (mixed * factor[None]).reshape(object_field.shape)


def solution(mesh):
    in_specs = (
        P("grp", None, "dev", None, None),
        P("grp", None, None),
        P(None, "dev", "grp", None),
    )
    out_specs = P(None, "dev", "grp", None)
    return jax.shard_map(
        per_device, mesh=mesh, in_specs=in_specs, out_specs=out_specs, check_vma=False
    )
```

time: 234 us -> 101 us (0.43)
  the two profiles are of different devices: /device:TPU:0 before, /device:TPU:24 now
where the time goes in v1:
time: 101 us
  Pallas kernels  96.6 us (96%)
  local copies, waits for them, and re-layouts  2.54 us (3%)
  other arithmetic  2.11 us (2%)
    pallas_call x1, Pallas kernels, per_device(): pl.pallas_call(kernel, out_shape=jax.ShapeDtypeStruct((2, quarter, column...  96.6 us
    unnamed x4, local copies, waits for them, and re-layouts  2.54 us

profile of v1, /device:TPU:24, one launch (start us, length us, event | category | flops | bytes accessed | tf_op | source)
XLA Modules:
  0.0 101.3 jit_solution(12137254734916632219)
XLA Ops:
  0.0 0.0 copy-start
  0.0 1.6 %copy-done = f32[2,1,256,1024]{3,2,1,0:T(8,128)S(1)} copy-done((f32[2,1,256,1024]{3,2,1,0:T(8,128)S(1)}, f32[2,1,256,1024]{3,2,1,0:T(8,128)}, u32[]{:S(2)}) %copy-start) | copy-done | bytes 2097176
  1.6 0.0 copy-start.1
  1.6 0.9 copy-done.1
  2.5 96.6 %shard_map.46 = f32[2,256,1024]{2,1,0:T(8,128)S(1)} custom-call(f32[256,256]{1,0:T(8,128)S(1)} %copy-done.1, f32[2,2,2,256,1024]{4,3,2,1,0:T(8,128)} %bitcast.10, f32[2,2,256,1024]{3,2,1,0:T(8,128)} %bitcast.11, f32[2,256,1024]{2,1,0:T(8,128)S(1)} %bitcast.9), custom_call_target="tpu_custom_call" | custom-call | tf_op jit(solution)/shard_map/pallas_call | solution.py:222
  99.2 0.5 divide_bitcast_fusion
  99.6 1.7 %multiply_bitcast_fusion = f32[2,1,256,1024]{3,2,1,0:T(8,128)} fusion(f32[2,256,1024]{2,1,0:T(8,128)S(1)} %shard_map.46, f32[256,1024]{1,0:T(8,128)S(1)} %divide_bitcast_fusion), kind=kLoop, calls=%fused_computation | loop fusion | flops 524288 | bytes 5242880 | tf_op jit(solution)/shard_map/reshape | solution.py:253
Async XLA Ops:
  0.0 1.6 %copy-start = (f32[2,1,256,1024]{3,2,1,0:T(8,128)S(1)}, f32[2,1,256,1024]{3,2,1,0:T(8,128)}, u32[]{:S(2)}) copy-start(f32[2,1,256,1024]{3,2,1,0:T(8,128)} %param.6) | copy-start | bytes 6291460
  1.6 0.9 copy-start.1

commit v2 on v1

v2 whole, which is shorter than its diff:
```python
import functools
import math

import jax
import jax.numpy as jnp
import numpy as np
from jax import lax
from jax.experimental import pallas as pl
from jax.experimental.pallas import tpu as pltpu
from jax.sharding import PartitionSpec as P

damping = 0.05
ceiling = 0.4
MESH = pl.DeviceIdType.MESH
CHUNKS = 4
PLAN = (
    ("sum", 0),
    ("ed", 0),
    ("eb", 0),
    ("dr", 0),
    ("sum", 1),
    ("ed", 1),
    ("damp", 0),
    ("sum", 2),
    ("sum", 3),
    ("wd", 0),
    ("wf", 0),
    ("ea", 0),
    ("eb", 1),
    ("wd", 1),
    ("wf", 1),
    ("ea", 1),
    ("wf", 2),
    ("wf", 3),
    ("ed", 2),
    ("eb", 2),
    ("ea", 2),
    ("ed", 3),
    ("eb", 3),
    ("ea", 3),
    ("wm", 0),
    ("ep", 0),
    ("ep", 1),
    ("em", 0),
    ("er", 0),
    ("ep", 2),
    ("em", 1),
    ("er", 1),
    ("ep", 3),
    ("hop", 0),
    ("em", 2),
    ("er", 2),
    ("hop", 1),
    ("em", 3),
    ("er", 3),
    ("hop", 2),
    ("hop", 3),
)


def mixing_matrix(count, lanes):
    wavenumber = np.arange(count)
    signed = np.where(2 * wavenumber < count, wavenumber, wavenumber - count)
    taper = np.exp(-((signed / (count / 8.0)) ** 2))
    offsets = (wavenumber[:, None] - wavenumber[None, :]) % count
    angles = 2.0 * math.pi / count * ((wavenumber[None, None, :] * offsets[:, :, None]) % count)
    mixing = np.sum(taper * np.cos(angles), axis=2) / count
    rows = mixing.reshape(4, 2, 4, count).transpose(1, 0, 2, 3).reshape(2, 16, count)
    return np.stack([np.kron(half, np.eye(lanes)) for half in rows]).astype(np.float32)


def wait_for(ref, sem):
    pltpu.make_async_copy(ref, ref, sem).wait()


def kernel(
    mix_hbm, grad, light, field, out,
    mix_ref, pbuf, cbuf, obuf, lbuf, dbuf, from_a, from_b, from_d, sbuf, xbuf, ybuf, rbuf,
    mix_sem, load_sem, field_sem, core_send, core_recv, light_send, light_recv,
    damp_send, damp_recv, y_send, y_recv, plane_send, plane_recv, back_send, back_recv,
    hop_send, hop_recv,
):
    width = pbuf.shape[-1]
    g = lax.axis_index("grp")
    me = lax.axis_index("dev")
    yh, core = lax.div(g, 2), lax.rem(g, 2)
    x, yl, z = lax.div(me, 8), lax.rem(lax.div(me, 4), 2), lax.rem(me, 4)
    place = x * 4 + z
    other_half = (1 - yh) * 2
    across = x * 8 + (1 - yl) * 4 + z

    sibling = (yh * 2 + 1 - core, me)
    a_side = (g, across)
    b_side = (other_half + core, across)
    b_cross = (other_half + 1 - core, across)
    d_side = (other_half + core, me)

    def plane_peer(i):
        return lax.rem(x + lax.rem(i, 4), 4), lax.rem(z + i + lax.div(i, 4), 4)

    def columns(k):
        return pl.ds(k * width, width)

    def remote(src, dst, send, recv, target):
        pltpu.make_async_remote_copy(
            src_ref=src, dst_ref=dst, send_sem=send, recv_sem=recv,
            device_id=target, device_id_type=MESH,
        ).start()

    order = list(range(CHUNKS))

    rows16 = pl.ds(pl.multiple_of(place * 16, 16), 16)
    pltpu.make_async_copy(light.at[yh, core, rows16], lbuf.at[0], light_recv).start()
    for k in order:
        pltpu.make_async_copy(
            grad.at[:, :, core, :, columns(k)], pbuf.at[k], load_sem.at[k]
        ).start()
    for k in order:
        pltpu.make_async_copy(field.at[:, :, columns(k)], obuf.at[k], field_sem.at[k]).start()
    pltpu.make_async_copy(mix_hbm, mix_ref, mix_sem).start()

    barrier = pltpu.get_barrier_semaphore()
    for target in (sibling, a_side, b_side, b_cross, d_side):
        pl.semaphore_signal(barrier, 1, device_id=target, device_id_type=MESH)

    def greet(i, carry):
        px, pz = plane_peer(i)
        pl.semaphore_signal(
            barrier, 1, device_id=(g, px * 8 + yl * 4 + pz), device_id_type=MESH
        )
        return carry

    lax.fori_loop(1, 16, greet, 0)
    pl.semaphore_wait(barrier, 20)

    remote(light.at[yh, 1 - core, rows16], lbuf.at[1], light_send, light_recv, sibling)
    remote(light.at[1 - yh, core, rows16], lbuf.at[2], light_send, light_recv, b_side)
    remote(light.at[1 - yh, 1 - core, rows16], lbuf.at[3], light_send, light_recv, b_cross)

    for k in order:
        remote(
            grad.at[:, :, 1 - core, :, columns(k)], cbuf.at[k],
            core_send, core_recv.at[k], sibling,
        )

    mine = pl.ds(pl.multiple_of(yl * 128, 128), 128)
    theirs = pl.ds(pl.multiple_of((1 - yl) * 128, 128), 128)

    def damp_of(k, which):
        wide = dbuf.shape[-1]
        half, start = k * width // wide, k * width % wide
        cols = slice(start, start + width)
        if which == "all":
            return dbuf[half, :, :, :, cols].reshape(256, width)
        if which == "mine":
            return dbuf[half, pl.ds(yl * 2, 2), :, :, cols].reshape(128, width)
        if which == "theirs":
            return dbuf[half, pl.ds((1 - yl) * 2, 2), :, :, cols].reshape(128, width)
        row = yl * 128 + place * 8
        return dbuf[half, lax.div(row, 64), lax.rem(lax.div(row, 16), 4),
                    pl.ds(pl.multiple_of(lax.rem(row, 16), 8), 8), cols]

    def chip_sum(k):
        wait_for(pbuf.at[k], load_sem.at[k])
        wait_for(cbuf.at[k], core_recv.at[k])
        pbuf[k] = pbuf[k] + cbuf[k]

    def early_d_send(k):
        remote(pbuf.at[k, :, 1 - yh, mine], from_d.at[k], y_send.at[0], y_recv.at[0, k], d_side)

    def early_b_send(k):
        remote(pbuf.at[k, :, 1 - yh, theirs], from_b.at[k], y_send.at[1], y_recv.at[1, k], b_side)

    def early_a_send(k):
        damp = damp_of(k, 'theirs')
        pbuf[k, :, yh, theirs] = obuf[k, :, theirs, :] * damp[None] - pbuf[k, :, yh, theirs]
        remote(pbuf.at[k, :, yh, theirs], from_a.at[k], y_send.at[2], y_recv.at[2, k], a_side)

    def ring(coordinate, i):
        return lax.rem(coordinate + i, 4)

    def reduce_damp():
        wait_for(lbuf, light_recv)
        total = lbuf[0] + lbuf[1] + lbuf[2] + lbuf[3] + damping
        wide = dbuf.shape[-1]
        for half in range(2):
            dbuf[half, x, z] = total[:, half * wide:(half + 1) * wide]
        for i in range(1, 4):
            remote(
                dbuf.at[0, x, z], dbuf.at[0, x, z], damp_send.at[0], damp_recv.at[0],
                (g, x * 8 + yl * 4 + ring(z, i)),
            )
            remote(
                dbuf.at[1, x, z], dbuf.at[1, x, z], damp_send.at[1], damp_recv.at[1],
                (g, ring(x, i) * 8 + yl * 4 + z),
            )

    def spread_damp():
        wait_for(dbuf.at[0, 0, pl.ds(0, 3)], damp_recv.at[0])
        for i in range(1, 4):
            remote(
                dbuf.at[0, x], dbuf.at[0, x], damp_send.at[2], damp_recv.at[2],
                (g, ring(x, i) * 8 + yl * 4 + z),
            )
        wait_for(dbuf.at[1, 0, pl.ds(0, 3)], damp_recv.at[1])
        for i in range(1, 4):
            remote(
                dbuf.at[1, :, z], dbuf.at[1, :, z], damp_send.at[3], damp_recv.at[3],
                (g, x * 8 + yl * 4 + ring(z, i)),
            )

    def wait_damp(half):
        wait_for(dbuf.at[half, pl.ds(0, 3)], damp_recv.at[2 + half])

    def mix(half, block):
        return jnp.dot(
            mix_ref[half], block, precision=lax.Precision.HIGHEST,
            preferred_element_type=jnp.float32,
        ).reshape(16, 8, width)

    def early_plane(k):
        damp = damp_of(k, 'mine')
        wait_for(from_d.at[k], y_recv.at[0, k])
        sbuf[k, :, yl] = obuf[k, :, mine, :] * damp[None] - pbuf[k, :, yh, mine] - from_d[k]
        wait_for(from_b.at[k], y_recv.at[1, k])
        wait_for(from_a.at[k], y_recv.at[2, k])
        sbuf[k, :, 1 - yl] = from_a[k] - from_b[k]

        def send(i, carry):
            px, pz = plane_peer(i)
            rows = pl.ds(pl.multiple_of((px * 4 + pz) * 8, 8), 8)
            remote(
                sbuf.at[k, :, :, rows], xbuf.at[k, :, x, :, z], plane_send, plane_recv.at[k],
                (g, px * 8 + yl * 4 + pz),
            )
            return carry

        lax.fori_loop(1, 16, send, 0)
        own = pl.ds(pl.multiple_of(place * 8, 8), 8)
        pltpu.make_async_copy(
            sbuf.at[k, :, :, own], xbuf.at[k, :, x, :, z], plane_recv.at[k]
        ).start()

    def early_mix(k):
        wait_for(xbuf.at[k], plane_recv.at[k])
        inverse = 1.0 / damp_of(k, 'early')
        for half in range(2):
            real, imag = (
                mix(half, xbuf[k, part].reshape(256, width)) * inverse[None] for part in range(2)
            )
            amplitude = jnp.sqrt(real * real + imag * imag)
            factor = ceiling / jnp.maximum(amplitude, ceiling)
            real, imag = real * factor, imag * factor
            ybuf[k, 0, half] = real
            ybuf[k, 1, half] = imag

    def early_return(k):
        rows = pl.ds(pl.multiple_of(place * 8, 8), 8)

        def send(i, carry):
            px, pz = plane_peer(i)
            remote(
                ybuf.at[k, :, :, px * 4 + pz], rbuf.at[k, :, :, rows], back_send, back_recv.at[k],
                (g, px * 8 + yl * 4 + pz),
            )
            return carry

        lax.fori_loop(1, 16, send, 0)
        pltpu.make_async_copy(
            ybuf.at[k, :, :, place], rbuf.at[k, :, :, rows], back_recv.at[k]
        ).start()

    def hop(k):
        wait_for(rbuf.at[k], back_recv.at[k])
        remote(
            rbuf.at[k, :, 1 - yl], out.at[:, mine, columns(k)], hop_send, hop_recv, a_side
        )
        pltpu.make_async_copy(
            rbuf.at[k, :, yl], out.at[:, mine, columns(k)], hop_recv
        ).start()

    steps = {
        "sum": chip_sum, "ed": early_d_send, "eb": early_b_send, "ea": early_a_send,
        "dr": lambda k: reduce_damp(), "damp": lambda k: spread_damp(), "wd": wait_damp,
        "ep": early_plane, "em": early_mix, "er": early_return, "hop": hop,
        "wm": lambda k: wait_for(mix_ref, mix_sem),
        "wf": lambda k: wait_for(obuf.at[k], field_sem.at[k]),
    }
    for name, k in PLAN:
        steps[name](k)

    wait_for(lbuf.at[pl.ds(0, 3)], light_send)
    wait_for(cbuf, core_send)
    wait_for(dbuf.at[0, 0, pl.ds(0, 3)], damp_send.at[0])
    wait_for(dbuf.at[0, 0, pl.ds(0, 3)], damp_send.at[1])
    wait_for(dbuf.at[0, pl.ds(0, 3)], damp_send.at[2])
    wait_for(dbuf.at[0, pl.ds(0, 3)], damp_send.at[3])
    wait_for(from_d, y_send.at[0])
    wait_for(from_b, y_send.at[1])
    wait_for(from_a, y_send.at[2])
    wait_for(sbuf.at[:, :, :, pl.ds(0, 120)], plane_send)
    wait_for(rbuf.at[:, :, :, pl.ds(0, 120)], back_send)
    wait_for(rbuf.at[:, :, 0], hop_send)
    wait_for(out, hop_recv)


def per_device(grad_parts, light_parts, object_field):
    rows, columns = light_parts.shape[1:]
    slices = 32
    quarter = rows // 4
    half = quarter // 2
    width = columns // CHUNKS
    f32 = jnp.float32
    grad = grad_parts.reshape(2, 2, 2, quarter, columns)
    light = light_parts.reshape(2, 2, quarter, columns)
    field = object_field.reshape(2, quarter, columns)
    matrix = jnp.asarray(mixing_matrix(slices, 8))
    in_hbm = pl.BlockSpec(memory_space=pltpu.HBM)
    in_vmem = pl.BlockSpec(memory_space=pltpu.VMEM)
    dma = pltpu.SemaphoreType.DMA
    updated = pl.pallas_call(
        kernel,
        out_shape=jax.ShapeDtypeStruct((2, quarter, columns), f32),
        in_specs=[in_hbm] * 4,
        out_specs=in_vmem,
        scratch_shapes=[
            pltpu.VMEM(matrix.shape, f32),
            pltpu.VMEM((CHUNKS, 2, 2, quarter, width), f32),
            pltpu.VMEM((CHUNKS, 2, 2, quarter, width), f32),
            pltpu.VMEM((CHUNKS, 2, quarter, width), f32),
            pltpu.VMEM((4, 16, columns), f32),
            pltpu.VMEM((2, 4, 4, quarter // 16, columns // 2), f32),
            pltpu.VMEM((CHUNKS, 2, half, width), f32),
            pltpu.VMEM((CHUNKS, 2, half, width), f32),
            pltpu.VMEM((CHUNKS, 2, half, width), f32),
            pltpu.VMEM((CHUNKS, 2, 2, half, width), f32),
            pltpu.VMEM((CHUNKS, 2, 4, 2, 4, 8, width), f32),
            pltpu.VMEM((CHUNKS, 2, 2, slices // 2, 8, width), f32),
            pltpu.VMEM((CHUNKS, 2, 2, half, width), f32),
            dma, dma((CHUNKS,)), dma((CHUNKS,)),
            dma, dma((CHUNKS,)),
            dma, dma,
            dma((4,)), dma((4,)),
            dma((3,)), dma((3, CHUNKS)),
            dma, dma((CHUNKS,)),
            dma, dma((CHUNKS,)),
            dma, dma,
        ],
        compiler_params=pltpu.CompilerParams(
            collective_id=0, has_side_effects=True, vmem_limit_bytes=48 * 2**20
        ),
    )(matrix, grad, light, field)
    return updated.reshape(object_field.shape)


def solution(mesh):
    in_specs = (
        P("grp", None, "dev", None, None),
        P("grp", None, None),
        P(None, "dev", "grp", None),
    )
    out_specs = P(None, "dev", "grp", None)
    return jax.shard_map(
        per_device, mesh=mesh, in_specs=in_specs, out_specs=out_specs, check_vma=False
    )
```

time: 101 us -> 93.3 us (0.924)
  the two profiles are of different devices: /device:TPU:24 before, /device:TPU:0 now
where the time goes in v2:
time: 93.3 us; the launch traced here: 92 us
  Pallas kernels  88.1 us (94%)
  local copies, waits for them, and re-layouts  3.86 us (4%)
    pallas_call x1, Pallas kernels, per_device(): pl.pallas_call(kernel, out_shape=jax.ShapeDtypeStruct((2, quarter, column...  88.1 us
    unnamed x5, local copies, waits for them, and re-layouts  3.86 us

profile of v2, /device:TPU:0, one launch (start us, length us, event | category | flops | bytes accessed | tf_op | source)
XLA Modules:
  0.0 92.0 jit_solution(18211326423261569685)
XLA Ops:
  0.0 0.0 copy-start
  0.0 1.6 %copy-done = f32[2,1,256,1024]{3,2,1,0:T(8,128)S(1)} copy-done((f32[2,1,256,1024]{3,2,1,0:T(8,128)S(1)}, f32[2,1,256,1024]{3,2,1,0:T(8,128)}, u32[]{:S(2)}) %copy-start) | copy-done | bytes 2097176
  1.6 0.0 copy-start.1
  1.6 0.9 %copy-done.1 = f32[2,128,256]{2,1,0:T(8,128)S(1)} copy-done((f32[2,128,256]{2,1,0:T(8,128)S(1)}, f32[2,128,256]{2,1,0:T(8,128)}, u32[]{:S(2)}) %copy-start.1) | copy-done | bytes 262168
  2.5 88.1 %shard_map.46 = f32[2,256,1024]{2,1,0:T(8,128)S(1)} custom-call(f32[2,128,256]{2,1,0:T(8,128)S(1)} %copy-done.1, f32[2,2,2,256,1024]{4,3,2,1,0:T(8,128)} %bitcast.8, f32[2,2,256,1024]{3,2,1,0:T(8,128)} %bitcast.9, f32[2,256,1024]{2,1,0:T(8,128)S(1)} %bitcast.7), custom_call_target="tpu_custom_call" | custom-call | tf_op jit(solution)/shard_map/pallas_call | solution.py:321
  90.7 1.3 %copy.7 = f32[2,1,256,1024]{3,2,1,0:T(8,128)} copy(f32[2,1,256,1024]{3,2,1,0:T(8,128)S(1)} %bitcast.6) | data formatting | bytes 4194304
Async XLA Ops:
  0.0 1.6 %copy-start = (f32[2,1,256,1024]{3,2,1,0:T(8,128)S(1)}, f32[2,1,256,1024]{3,2,1,0:T(8,128)}, u32[]{:S(2)}) copy-start(f32[2,1,256,1024]{3,2,1,0:T(8,128)} %param.6) | copy-start | bytes 6291460
  1.6 0.9 %copy-start.1 = (f32[2,128,256]{2,1,0:T(8,128)S(1)}, f32[2,128,256]{2,1,0:T(8,128)}, u32[]{:S(2)}) copy-start(f32[2,128,256]{2,1,0:T(8,128)} %constant.2.clone.mix_hbm) | copy-start | bytes 786436

commit v3 on v2

v3 whole, which is shorter than its diff:
```python
import functools
import math

import jax
import jax.numpy as jnp
import numpy as np
from jax import lax
from jax.experimental import pallas as pl
from jax.experimental.pallas import tpu as pltpu
from jax.sharding import PartitionSpec as P

damping = 0.05
ceiling = 0.4
MESH = pl.DeviceIdType.MESH
WIDTHS = (256, 256, 256, 128, 128)
CHUNKS = len(WIDTHS)
PLAN = (
    ("sum", 0),
    ("ed", 0),
    ("eb", 0),
    ("dr", 0),
    ("sum", 1),
    ("ed", 1),
    ("damp", 0),
    ("sum", 2),
    ("sum", 3),
    ("sum", 4),
    ("wd", 0),
    ("wf", 0),
    ("ea", 0),
    ("eb", 1),
    ("wd", 1),
    ("wf", 1),
    ("wf", 2),
    ("wf", 3),
    ("wf", 4),
    ("ea", 1),
    ("ed", 2),
    ("eb", 2),
    ("ea", 2),
    ("ed", 3),
    ("eb", 3),
    ("ea", 3),
    ("ed", 4),
    ("eb", 4),
    ("ea", 4),
    ("ep", 0),
    ("ep", 1),
    ("em", 0),
    ("er", 0),
    ("ep", 2),
    ("em", 1),
    ("er", 1),
    ("ep", 3),
    ("em", 2),
    ("er", 2),
    ("ep", 4),
    ("hop", 0),
    ("hop", 1),
    ("em", 3),
    ("er", 3),
    ("hop", 2),
    ("em", 4),
    ("er", 4),
    ("hop", 3),
    ("hop", 4),
)


def mixing_row(count):
    wavenumber = np.arange(count)
    signed = np.where(2 * wavenumber < count, wavenumber, wavenumber - count)
    taper = np.exp(-((signed / (count / 8.0)) ** 2))
    angles = 2.0 * math.pi / count * (wavenumber[None, :] * wavenumber[:, None] % count)
    return [float(value) for value in np.sum(taper * np.cos(angles), axis=1) / count]


def mixing_matrix(half):
    shape = (128, 256)
    row, column = (lax.broadcasted_iota(jnp.int32, shape, axis) for axis in range(2))
    out = (row // 32) * 8 + half * 4 + (row // 8) % 4
    apart = jnp.abs(out - column // 8)
    apart = jnp.where(row % 8 == column % 8, jnp.minimum(apart, 32 - apart), -1)
    values = mixing_row(32)
    matrix = jnp.zeros(shape, jnp.float32)
    for distance in range(17):
        matrix = jnp.where(apart == distance, values[distance], matrix)
    return matrix


def wait_for(ref, sem):
    pltpu.make_async_copy(ref, ref, sem).wait()


def kernel(
    grad, light, field, out,
    mix_ref, pbuf, cbuf, obuf, lbuf, dbuf, from_a, from_b, from_d, sbuf, xbuf, ybuf, rbuf,
    load_sem, field_sem, core_send, core_recv, light_send, light_recv,
    damp_send, damp_recv, y_send, y_recv, plane_send, plane_recv, back_send, back_recv,
    hop_send, hop_recv,
):
    g = lax.axis_index("grp")
    me = lax.axis_index("dev")
    yh, core = lax.div(g, 2), lax.rem(g, 2)
    x, yl, z = lax.div(me, 8), lax.rem(lax.div(me, 4), 2), lax.rem(me, 4)
    place = x * 4 + z
    other_half = (1 - yh) * 2
    across = x * 8 + (1 - yl) * 4 + z

    sibling = (yh * 2 + 1 - core, me)
    a_side = (g, across)
    b_side = (other_half + core, across)
    b_cross = (other_half + 1 - core, across)
    d_side = (other_half + core, me)

    def plane_peer(i):
        return lax.rem(x + lax.rem(i, 4), 4), lax.rem(z + i + lax.div(i, 4), 4)

    def columns(k):
        return pl.ds(sum(WIDTHS[:k]), WIDTHS[k])

    def remote(src, dst, send, recv, target):
        pltpu.make_async_remote_copy(
            src_ref=src, dst_ref=dst, send_sem=send, recv_sem=recv,
            device_id=target, device_id_type=MESH,
        ).start()

    order = list(range(CHUNKS))

    rows16 = pl.ds(pl.multiple_of(place * 16, 16), 16)
    pltpu.make_async_copy(light.at[yh, core, rows16], lbuf.at[0], light_recv).start()
    for k in order:
        pltpu.make_async_copy(
            grad.at[:, :, core, :, columns(k)], pbuf[k], load_sem.at[k]
        ).start()
    for k in order:
        pltpu.make_async_copy(field.at[:, :, columns(k)], obuf[k], field_sem.at[k]).start()

    barrier = pltpu.get_barrier_semaphore()
    for target in (sibling, a_side, b_side, b_cross, d_side):
        pl.semaphore_signal(barrier, 1, device_id=target, device_id_type=MESH)

    def greet(i, carry):
        px, pz = plane_peer(i)
        pl.semaphore_signal(
            barrier, 1, device_id=(g, px * 8 + yl * 4 + pz), device_id_type=MESH
        )
        return carry

    lax.fori_loop(1, 16, greet, 0)
    for half in range(2):
        mix_ref[half] = mixing_matrix(half)
    pl.semaphore_wait(barrier, 20)

    remote(light.at[yh, 1 - core, rows16], lbuf.at[1], light_send, light_recv, sibling)
    remote(light.at[1 - yh, core, rows16], lbuf.at[2], light_send, light_recv, b_side)
    remote(light.at[1 - yh, 1 - core, rows16], lbuf.at[3], light_send, light_recv, b_cross)

    for k in order:
        remote(
            grad.at[:, :, 1 - core, :, columns(k)], cbuf[k],
            core_send.at[k], core_recv.at[k], sibling,
        )

    mine = pl.ds(pl.multiple_of(yl * 128, 128), 128)
    theirs = pl.ds(pl.multiple_of((1 - yl) * 128, 128), 128)

    def damp_of(k, which):
        wide = dbuf.shape[-1]
        width = WIDTHS[k]
        half, start = sum(WIDTHS[:k]) // wide, sum(WIDTHS[:k]) % wide
        cols = slice(start, start + width)
        if which == "all":
            return dbuf[half, :, :, :, cols].reshape(256, width)
        if which == "mine":
            return dbuf[half, pl.ds(yl * 2, 2), :, :, cols].reshape(128, width)
        if which == "theirs":
            return dbuf[half, pl.ds((1 - yl) * 2, 2), :, :, cols].reshape(128, width)
        row = yl * 128 + place * 8
        return dbuf[half, lax.div(row, 64), lax.rem(lax.div(row, 16), 4),
                    pl.ds(pl.multiple_of(lax.rem(row, 16), 8), 8), cols]

    def chip_sum(k):
        wait_for(pbuf[k], load_sem.at[k])
        wait_for(cbuf[k], core_recv.at[k])
        pbuf[k][...] = pbuf[k][...] + cbuf[k][...]

    def early_d_send(k):
        remote(pbuf[k].at[:, 1 - yh, mine], from_d[k], y_send.at[0, k], y_recv.at[0, k], d_side)

    def early_b_send(k):
        remote(pbuf[k].at[:, 1 - yh, theirs], from_b[k], y_send.at[1, k], y_recv.at[1, k], b_side)

    def early_a_send(k):
        damp = damp_of(k, 'theirs')
        pbuf[k][:, yh, theirs] = obuf[k][:, theirs, :] * damp[None] - pbuf[k][:, yh, theirs]
        remote(pbuf[k].at[:, yh, theirs], from_a[k], y_send.at[2, k], y_recv.at[2, k], a_side)

    def ring(coordinate, i):
        return lax.rem(coordinate + i, 4)

    def reduce_damp():
        wait_for(lbuf, light_recv)
        total = lbuf[0] + lbuf[1] + lbuf[2] + lbuf[3] + damping
        wide = dbuf.shape[-1]
        for half in range(2):
            dbuf[half, x, z] = total[:, half * wide:(half + 1) * wide]
        for i in range(1, 4):
            remote(
                dbuf.at[0, x, z], dbuf.at[0, x, z], damp_send.at[0], damp_recv.at[0],
                (g, x * 8 + yl * 4 + ring(z, i)),
            )
            remote(
                dbuf.at[1, x, z], dbuf.at[1, x, z], damp_send.at[1], damp_recv.at[1],
                (g, ring(x, i) * 8 + yl * 4 + z),
            )

    def spread_damp():
        wait_for(dbuf.at[0, 0, pl.ds(0, 3)], damp_recv.at[0])
        for i in range(1, 4):
            remote(
                dbuf.at[0, x], dbuf.at[0, x], damp_send.at[2], damp_recv.at[2],
                (g, ring(x, i) * 8 + yl * 4 + z),
            )
        wait_for(dbuf.at[1, 0, pl.ds(0, 3)], damp_recv.at[1])
        for i in range(1, 4):
            remote(
                dbuf.at[1, :, z], dbuf.at[1, :, z], damp_send.at[3], damp_recv.at[3],
                (g, x * 8 + yl * 4 + ring(z, i)),
            )

    def wait_damp(half):
        wait_for(dbuf.at[half, pl.ds(0, 3)], damp_recv.at[2 + half])

    def mix(half, block):
        return jnp.dot(
            mix_ref[half], block, precision=lax.Precision.HIGHEST,
            preferred_element_type=jnp.float32,
        ).reshape(16, 8, block.shape[1])

    def early_plane(k):
        damp = damp_of(k, 'mine')
        wait_for(from_d[k], y_recv.at[0, k])
        sbuf[k][:, yl] = obuf[k][:, mine, :] * damp[None] - pbuf[k][:, yh, mine] - from_d[k][...]
        wait_for(from_b[k], y_recv.at[1, k])
        wait_for(from_a[k], y_recv.at[2, k])
        sbuf[k][:, 1 - yl] = from_a[k][...] - from_b[k][...]

        def send(i, carry):
            px, pz = plane_peer(i)
            rows = pl.ds(pl.multiple_of((px * 4 + pz) * 8, 8), 8)
            remote(
                sbuf[k].at[:, :, rows], xbuf[k].at[:, x, :, z], plane_send.at[k], plane_recv.at[k],
                (g, px * 8 + yl * 4 + pz),
            )
            return carry

        lax.fori_loop(1, 16, send, 0)
        own = pl.ds(pl.multiple_of(place * 8, 8), 8)
        pltpu.make_async_copy(
            sbuf[k].at[:, :, own], xbuf[k].at[:, x, :, z], plane_recv.at[k]
        ).start()

    def early_mix(k):
        wait_for(xbuf[k], plane_recv.at[k])
        inverse = 1.0 / damp_of(k, 'early')
        for half in range(2):
            real, imag = (
                mix(half, xbuf[k][part].reshape(256, WIDTHS[k])) * inverse[None] for part in range(2)
            )
            amplitude = jnp.sqrt(real * real + imag * imag)
            factor = ceiling / jnp.maximum(amplitude, ceiling)
            real, imag = real * factor, imag * factor
            ybuf[k][0, half] = real
            ybuf[k][1, half] = imag

    def early_return(k):
        rows = pl.ds(pl.multiple_of(place * 8, 8), 8)

        def send(i, carry):
            px, pz = plane_peer(i)
            remote(
                ybuf[k].at[:, :, px * 4 + pz], rbuf[k].at[:, :, rows], back_send.at[k], back_recv.at[k],
                (g, px * 8 + yl * 4 + pz),
            )
            return carry

        lax.fori_loop(1, 16, send, 0)
        pltpu.make_async_copy(
            ybuf[k].at[:, :, place], rbuf[k].at[:, :, rows], back_recv.at[k]
        ).start()

    def hop(k):
        wait_for(rbuf[k], back_recv.at[k])
        remote(
            rbuf[k].at[:, 1 - yl], out.at[:, mine, columns(k)], hop_send.at[k], hop_recv.at[k], a_side
        )
        pltpu.make_async_copy(
            rbuf[k].at[:, yl], out.at[:, mine, columns(k)], hop_recv.at[k]
        ).start()

    steps = {
        "sum": chip_sum, "ed": early_d_send, "eb": early_b_send, "ea": early_a_send,
        "dr": lambda k: reduce_damp(), "damp": lambda k: spread_damp(), "wd": wait_damp,
        "ep": early_plane, "em": early_mix, "er": early_return, "hop": hop,
        "wf": lambda k: wait_for(obuf[k], field_sem.at[k]),
    }
    for name, k in PLAN:
        steps[name](k)

    wait_for(lbuf.at[pl.ds(0, 3)], light_send)
    wait_for(dbuf.at[0, 0, pl.ds(0, 3)], damp_send.at[0])
    wait_for(dbuf.at[0, 0, pl.ds(0, 3)], damp_send.at[1])
    wait_for(dbuf.at[0, pl.ds(0, 3)], damp_send.at[2])
    wait_for(dbuf.at[0, pl.ds(0, 3)], damp_send.at[3])
    for k in range(CHUNKS):
        wait_for(cbuf[k], core_send.at[k])
        wait_for(from_d[k], y_send.at[0, k])
        wait_for(from_b[k], y_send.at[1, k])
        wait_for(from_a[k], y_send.at[2, k])
        wait_for(sbuf[k].at[:, :, pl.ds(0, 120)], plane_send.at[k])
        wait_for(rbuf[k].at[:, :, pl.ds(0, 120)], back_send.at[k])
        wait_for(rbuf[k].at[:, 0], hop_send.at[k])
        wait_for(out.at[:, :, columns(k)], hop_recv.at[k])


def per_device(grad_parts, light_parts, object_field):
    rows, columns = light_parts.shape[1:]
    slices = 32
    quarter = rows // 4
    half = quarter // 2
    f32 = jnp.float32
    grad = grad_parts.reshape(2, 2, 2, quarter, columns)
    light = light_parts.reshape(2, 2, quarter, columns)
    field = object_field.reshape(2, quarter, columns)
    in_hbm = pl.BlockSpec(memory_space=pltpu.HBM)
    in_vmem = pl.BlockSpec(memory_space=pltpu.VMEM)
    dma = pltpu.SemaphoreType.DMA

    def per_chunk(*shape):
        return tuple(pltpu.VMEM((*shape, width), f32) for width in WIDTHS)

    updated = pl.pallas_call(
        kernel,
        out_shape=jax.ShapeDtypeStruct((2, quarter, columns), f32),
        in_specs=[in_hbm] * 3,
        out_specs=in_vmem,
        scratch_shapes=[
            pltpu.VMEM((2, 128, 256), f32),
            per_chunk(2, 2, quarter),
            per_chunk(2, 2, quarter),
            per_chunk(2, quarter),
            pltpu.VMEM((4, 16, columns), f32),
            pltpu.VMEM((2, 4, 4, quarter // 16, columns // 2), f32),
            per_chunk(2, half),
            per_chunk(2, half),
            per_chunk(2, half),
            per_chunk(2, 2, half),
            per_chunk(2, 4, 2, 4, 8),
            per_chunk(2, 2, slices // 2, 8),
            per_chunk(2, 2, half),
            dma((CHUNKS,)), dma((CHUNKS,)),
            dma((CHUNKS,)), dma((CHUNKS,)),
            dma, dma,
            dma((4,)), dma((4,)),
            dma((3, CHUNKS)), dma((3, CHUNKS)),
            dma((CHUNKS,)), dma((CHUNKS,)),
            dma((CHUNKS,)), dma((CHUNKS,)),
            dma((CHUNKS,)), dma((CHUNKS,)),
        ],
        compiler_params=pltpu.CompilerParams(
            collective_id=0, has_side_effects=True, vmem_limit_bytes=51 * 2**20
        ),
    )(grad, light, field)
    return updated.reshape(object_field.shape)


def solution(mesh):
    in_specs = (
        P("grp", None, "dev", None, None),
        P("grp", None, None),
        P(None, "dev", "grp", None),
    )
    out_specs = P(None, "dev", "grp", None)
    return jax.shard_map(
        per_device, mesh=mesh, in_specs=in_specs, out_specs=out_specs, check_vma=False
    )
```

time: 93.3 us -> 88.1 us (0.944); the launches traced: 92 us -> 88 us
  local copies, waits for them, and re-layouts: 3.86 us -> 1.32 us
  Pallas kernels: 88.1 us -> 86.7 us
    unnamed x5 -> x1, local copies, waits for them, and re-layouts: 3.86 us -> 1.32 us
    pallas_call x1, Pallas kernels: 88.1 us -> 86.7 us  [per_device(): pl.pallas_call(kernel, out_shape=jax.ShapeDtypeStruct((2, quarter, column...]
where the time goes in v3:
time: 88.1 us; the launch traced here: 88 us
  Pallas kernels  86.7 us (98%)
  local copies, waits for them, and re-layouts  1.32 us (1%)
    pallas_call x1, Pallas kernels, per_device(): pl.pallas_call(kernel, out_shape=jax.ShapeDtypeStruct((2, quarter, column...  86.7 us

profile of v3, /device:TPU:0, one launch (start us, length us, event | category | flops | bytes accessed | tf_op | source)
XLA Modules:
  0.0 88.0 jit_solution(611856814046495961)
XLA Ops:
  0.0 86.7 %shard_map.37 = f32[2,256,1024]{2,1,0:T(8,128)S(1)} custom-call(f32[2,2,2,256,1024]{4,3,2,1,0:T(8,128)} %bitcast.7, f32[2,2,256,1024]{3,2,1,0:T(8,128)} %bitcast.8, f32[2,256,1024]{2,1,0:T(8,128)} %bitcast.9), custom_call_target="tpu_custom_call" | custom-call | tf_op jit(solution)/shard_map/pallas_call | solution.py:343
  86.7 1.3 %copy.6 = f32[2,1,256,1024]{3,2,1,0:T(8,128)} copy(f32[2,1,256,1024]{3,2,1,0:T(8,128)S(1)} %bitcast.6) | data formatting | bytes 4194304

commit v4 on v3

--- a/solution.py
+++ b/solution.py
@@ -39,10 +39,10 @@
     ("eb", 2),
     ("ea", 2),
     ("ed", 3),
+    ("ed", 4),
     ("eb", 3),
+    ("eb", 4),
     ("ea", 3),
-    ("ed", 4),
-    ("eb", 4),
     ("ea", 4),
     ("ep", 0),
     ("ep", 1),

time: 88.1 us -> 88.1 us (level)
  no operation moved by 1% of the time
where the time goes in v4:
time: 88.1 us; the launch traced here: 87.9 us
  Pallas kernels  86.5 us (98%)
  local copies, waits for them, and re-layouts  1.32 us (1%)
    pallas_call x1, Pallas kernels, per_device(): pl.pallas_call(kernel, out_shape=jax.ShapeDtypeStruct((2, quarter, column...  86.5 us

profile of v4, /device:TPU:0, one launch (start us, length us, event | category | flops | bytes accessed | tf_op | source)
XLA Modules:
  0.0 87.9 jit_solution(5657076469797963976)
XLA Ops:
  0.0 86.5 %shard_map.37 = f32[2,256,1024]{2,1,0:T(8,128)S(1)} custom-call(f32[2,2,2,256,1024]{4,3,2,1,0:T(8,128)} %bitcast.7, f32[2,2,256,1024]{3,2,1,0:T(8,128)} %bitcast.8, f32[2,256,1024]{2,1,0:T(8,128)} %bitcast.9), custom_call_target="tpu_custom_call" | custom-call | tf_op jit(solution)/shard_map/pallas_call | solution.py:343
  86.5 1.3 %copy.6 = f32[2,1,256,1024]{3,2,1,0:T(8,128)} copy(f32[2,1,256,1024]{3,2,1,0:T(8,128)S(1)} %bitcast.6) | data formatting | bytes 4194304
